TPU v7x, 32 devices: a whole 2x2x4 slice. The times are simulated.
32 devices in a mesh: dp: 16 (over z, y, x), tensor: 2 (over core).
Axes of the slice: x: 2, y: 2, z: 4, core: 2. Of those that a mesh axis runs over, the one named last changes fastest.
Arguments:
- inputs: bfloat16 [6144, 12288], P('dp', 'tensor'), may hold values from -160 to 160
- out_grad: bfloat16 [6144, 6144], P('dp'), may hold values from -0.08930431 to 0.08930431
- weight_codes: bfloat16 [6144, 12288], P('dp', 'tensor'), may hold values from -1 to 1
- weight_scales: bfloat16 [6144], P('dp'), may hold values from 0.0039978027 to 0.019897461
- master: float32 [6144, 12288], P('dp', 'tensor'), may hold values from -0.8 to 0.8
- moment: float32 [6144, 12288], P('dp', 'tensor'), may hold values from -3 to 3
- second: float32 [6144, 12288], P('dp', 'tensor'), may hold values from 0.05 to 0.5
Outputs:
- grad_input: bfloat16 [6144, 12288], P('dp', 'tensor')
- new_master: float32 [6144, 12288], P('dp', 'tensor')
- new_moment: float32 [6144, 12288], P('dp', 'tensor')
- new_second: float32 [6144, 12288], P('dp', 'tensor')
- new_codes: bfloat16 [6144, 12288], P('dp', 'tensor')
- new_scales: bfloat16 [6144], P('dp')
- grad_peak: float32 [], replicated
All inputs are finite; a program needn't handle non-finite values. Where the computation divides by a largest or mean magnitude, that divisor is 1e-20 or more.
Results may differ from a plain program's by a relative error of at most 0.019.
Values may be sent and summed in bfloat16 or wider, within the bound.
A program may use at most 512 MiB of HBM per device.

v0:
```python
import jax
import jax.numpy as jnp
from jax import lax
from jax.sharding import PartitionSpec as P

IN = 12288
OUT = 6144


def block_term(grads, acts):
    return lax.dot_general(
        grads, acts, (((0,), (0,)), ((), ())), preferred_element_type=jnp.float32
    )


def grid_round(partial_value, divisor):
    scaled = lax.optimization_barrier((partial_value / divisor * 64.0).astype(jnp.bfloat16))
    return scaled.astype(jnp.float32)


def on_device(inputs, out_grad, weight_codes, weight_scales, master, moment, second):
    weight = (
        lax.all_gather(weight_codes, "dp", axis=0, tiled=True).astype(jnp.float32)
        * lax.all_gather(weight_scales, "dp", axis=0, tiled=True).astype(jnp.float32)[:, None]
    ).astype(jnp.bfloat16)
    folded = jnp.dot(out_grad, weight, preferred_element_type=jnp.float32)
    grad_input = folded.astype(jnp.bfloat16)
    gradient_partial_value = block_term(out_grad, inputs)
    local_peak = jnp.max(jnp.abs(gradient_partial_value))
    grad_peak = lax.pmax(local_peak, ("dp", "tensor"))
    divisor = grad_peak + 1e-06
    summed = lax.psum_scatter(
        grid_round(gradient_partial_value, divisor).astype(jnp.bfloat16),
        "dp",
        scatter_dimension=0,
        tiled=True,
    ).astype(jnp.float32)
    gradient = summed * divisor / 64.0
    squares = lax.psum(jnp.sum(gradient * gradient), ("dp", "tensor"))
    clip_factor = jnp.minimum(1.0, jnp.sqrt(jnp.float32(OUT * IN)) / (jnp.sqrt(squares) + 1e-06))
    clipped = clip_factor * gradient
    new_moment = 0.9 * moment + 0.1 * clipped
    new_second = 0.95 * second + 0.05 * clipped * clipped
    new_master = master - 0.01 * (new_moment / (jnp.sqrt(new_second) + 1e-08) + 0.1 * master)
    row_peak = lax.pmax(jnp.max(jnp.abs(new_master), axis=1), "tensor") + 1e-06
    new_codes = (new_master / row_peak[:, None]).astype(jnp.bfloat16)
    new_scales = row_peak.astype(jnp.bfloat16)
    return (grad_input, new_master, new_moment, new_second, new_codes, new_scales, grad_peak)


def solution(mesh):
    return jax.shard_map(
        on_device,
        mesh=mesh,
        in_specs=(
            P("dp", "tensor"),
            P("dp", None),
            P("dp", "tensor"),
            P("dp"),
            P("dp", "tensor"),
            P("dp", "tensor"),
            P("dp", "tensor"),
        ),
        out_specs=(
            P("dp", "tensor"),
            P("dp", "tensor"),
            P("dp", "tensor"),
            P("dp", "tensor"),
            P("dp", "tensor"),
            P("dp"),
            P(),
        ),
        check_vma=False,
    )
```

profile of v0, /device:TPU:0, one launch (start us, length us, event | category | flops | bytes accessed | tf_op | source)
XLA Modules:
  0.0 1903.4 jit_solution(5723546318158391504)
XLA Ops:
  7.2 0.0 all-gather.3.cloned.1.call-start
  7.2 0.7 all-gather.3.cloned.1.call-update
  7.9 0.0 reduce-scatter.2.cloned.1.call-start
  7.9 64.6 %abs_reduce_fusion = (f32[]{:T(128)}, f32[6144,6144]{1,0:T(8,128)}) fusion(bf16[384,6144]{1,0:T(8,128)(2,1)} %param.8, bf16[384,6144]{1,0:T(8,128)(2,1)} %param.7), kind=kOutput, calls=%fused_computation.1 | convolution fusion | flops 29066526720 | bytes 160432128 | tf_op jit(solution)/shard_map/dot_general | solution.py:11
  72.6 47.2 %pmax.14 = f32[]{:T(128)} all-reduce(f32[]{:T(128)} %get-tuple-element.27), channel_id=1, replica_groups=mesh['dp'=16,'tensor'=2] {'dp','tensor'}, use_global_device_ids=true, to_apply=%region_1.0 | all-reduce | flops 1 | bytes 8 | tf_op jit(solution)/shard_map/pmax | solution.py:30
  120.4 74.3 %multiply_convert_fusion = bf16[6144,6144]{1,0:T(8,128)(2,1)} fusion(f32[6144,6144]{1,0:T(8,128)} %get-tuple-element.28, f32[]{:T(128)S(6)} %add.31), kind=kLoop, calls=%fused_computation | loop fusion | flops 113246208 | bytes 226492416 | tf_op jit(solution)/shard_map/convert_element_type | solution.py:17
  194.8 0.0 copy-start
  194.8 0.0 reduce-scatter.2.cloned.1.call-update
  194.8 0.7 copy-done
  195.5 41.7 %all-gather = bf16[16,1,384]{2,1,0:T(2,128)(2,1)S(1)} all-gather(bf16[1,1,384]{2,1,0:T(2,128)(2,1)S(1)} %reshape.16), channel_id=1, replica_groups=mesh['dp'=16,'tensor'=2] {'dp'}, dimensions={0}, use_global_device_ids=true | all-gather | bytes 13056 | tf_op jit(solution)/shard_map/all_gather | solution.py:24
  237.1 525.7 %all-gather.3.cloned.1.call-done = bf16[6144,6144]{1,0:T(8,128)(2,1)} async-done(((bf16[384,6144]{1,0:T(8,128)(2,1)}), bf16[6144,6144]{1,0:T(8,128)(2,1)}) %all-gather.3.cloned.1.call-update) | async-done | bytes 75497488 | tf_op jit(solution)/shard_map/all_gather | solution.py:23
  762.9 53.0 %fusion.5 = bf16[384,6144]{0,1:T(8,128)(2,1)} fusion(bf16[384,6144]{1,0:T(8,128)(2,1)} %param.8, bf16[6144,6144]{1,0:T(8,128)(2,1)} %all-gather.3.cloned.1.call-done, f32[6144]{0:T(1024)S(1)} %bitcast.6), kind=kOutput, calls=%fused_computation.15 | convolution fusion | flops 29106634752 | bytes 84959232 | tf_op jit(solution)/shard_map/dot_general | solution.py:26
  815.9 993.7 %reduce-scatter.2.cloned.1.call-done = bf16[384,6144]{1,0:T(8,128)(2,1)} async-done(((bf16[6144,6144]{1,0:T(8,128)(2,1)}), bf16[384,6144]{1,0:T(8,128)(2,1)}) %reduce-scatter.2.cloned.1.call-update) | async-done | bytes 4718608 | tf_op jit(solution)/shard_map/reduce_scatter | solution.py:32
  1809.6 5.4 multiply_reduce_fusion
  1815.0 6.6 copy.15
  1821.6 39.8 %psum.7 = f32[]{:T(128)} all-reduce(f32[]{:T(128)} %multiply_reduce_fusion), channel_id=1, replica_groups=mesh['dp'=16,'tensor'=2] {'dp','tensor'}, use_global_device_ids=true, to_apply=%region_4.0 | all-reduce | flops 1 | bytes 8 | tf_op jit(solution)/shard_map/psum | solution.py:39
  1862.1 24.2 %abs_reduce_fusion.1 = (f32[384]{0:T(512)S(1)}, f32[384,6144]{1,0:T(8,128)}, f32[384,6144]{1,0:T(8,128)}, f32[384,6144]{1,0:T(8,128)}) fusion(f32[384,6144]{1,0:T(8,128)} %param.11, f32[]{:T(128)S(6)} %mul.73, f32[]{:T(128)S(6)} %add.31, bf16[384,6144]{1,0:T(8,128)(2,1)} %reduce-scatter.2.cloned.1.call-done, f32[384,6144]{1,0:T(8,128)} %param.13, ...), kind=kLoop, calls=%fused_computation.8 | loop fusion | flops 42466944 | bytes 61343240 | tf_op jit(solution)/shard_map/reduce_max | solution.py:45
  1886.3 2.4 pmax.15
  1888.8 0.6 fusion.6
  1889.3 7.2 divide_convert_fusion
  (2 shorter events, 0.0 us)
Async XLA Ops:
  7.2 755.7 %all-gather.3.cloned.1.call-start = ((), (), s32[]{:S(2)}) async-start(), calls=%async_computation.1 | async-start | bytes 80216064 | tf_op jit(solution)/shard_map/all_gather | solution.py:23
  7.9 1801.7 %reduce-scatter.2.cloned.1.call-start = ((), (), s32[]{:S(2)}) async-start(), calls=%async_computation.2 | async-start | bytes 80216064 | tf_op jit(solution)/shard_map/reduce_scatter | solution.py:32
  194.8 0.7 copy-start
Sparse Core Ops, SparseCore 0:
  10.9 751.9 all-gather.2
  768.9 1040.6 reduce-scatter.1
where the time goes:
time: 1900 us
  waiting for transfers between devices  1520 us (80%)
  blocking collectives  131 us (7%)
  matrix products  118 us (6%)
  other arithmetic  112 us (6%)
    reduce_scatter x1, waiting for transfers between devices, on_device(): lax.psum_scatter(grid_round(gradient_partial_value, divisor).astype(jnp.b...  994 us
    all_gather x1, waiting for transfers between devices, on_device(): lax.all_gather(weight_codes, 'dp', axis=0, tiled=True).astype(jnp.float32)  526 us
    convert_element_type x1, other arithmetic, grid_round(): (partial_value / divisor * 64.0).astype(jnp.bfloat16)  74.3 us
    dot_general x1, matrix products, block_term(): lax.dot_general(grads, acts, (((0,), (0,)), ((), ())), preferred_element_...  64.6 us
    dot_general x1, matrix products, on_device(): folded = jnp.dot(out_grad, weight, preferred_element_type=jnp.float32)  53 us
    pmax x1, blocking collectives, on_device(): grad_peak = lax.pmax(local_peak, ('dp', 'tensor'))  47.2 us
    all_gather x1, blocking collectives, on_device(): lax.all_gather(weight_scales, 'dp', axis=0, tiled=True).astype(jnp.float32)  41.7 us
    psum x1, blocking collectives, on_device(): squares = lax.psum(jnp.sum(gradient * gradient), ('dp', 'tensor'))  39.8 us
  transfers between devices with their start and end apart: 2, of which 2 were waited for; matrix products, arithmetic and copies ran while one was open for 10% of the time, Pallas kernels for 0%

commit v1 on v0

v1 whole, which is shorter than its diff:
```python
import math

import jax
import jax.numpy as jnp
from jax import lax
from jax.sharding import PartitionSpec as P


def inner_size(n):
    for size in range(math.isqrt(n), 0, -1):
        if n % size == 0:
            return n // size
    return n


def on_device(n, inputs, out_grad, weight_codes, weight_scales, master, moment, second):
    inner = inner_size(n)
    outer = n // inner
    lines_of = [[a * inner + b for a in range(outer)] for b in range(inner)]
    tok = inputs.shape[0]
    own = weight_codes.shape[0]
    cols = inputs.shape[1]
    place = lax.rem(lax.axis_index("dp"), inner)
    paired = inner & (inner - 1) == 0

    def partner(b, step):
        return b ^ step if paired else (inner + step - b) % inner

    def swap(value, step):
        pairs = [(a * inner + b, a * inner + partner(b, step)) for a in range(outer) for b in range(inner)]
        return lax.ppermute(value, "dp", pairs)

    def moves(step):
        return step > 0 or not paired

    weight = (weight_codes.astype(jnp.float32) * weight_scales.astype(jnp.float32)[:, None]).astype(jnp.bfloat16)
    weight = lax.all_gather(weight, "dp", axis=0, tiled=True, axis_index_groups=lines_of)

    blocks = out_grad.reshape(tok, outer, inner, own).transpose(2, 0, 1, 3).reshape(inner, tok, outer * own)
    grads = []
    acts = []
    for step in range(inner):
        block = lax.dynamic_index_in_dim(blocks, partner(place, step), 0, keepdims=False)
        grads.append(swap(block, step) if moves(step) else block)
    for step in range(inner):
        acts.append(swap(inputs, step) if moves(step) else inputs)

    total = None
    peak = None
    for block, act in zip(grads, acts):
        term = lax.dot_general(
            block, act, (((0,), (0,)), ((), ())), preferred_element_type=jnp.float32
        )
        high = jnp.max(jnp.abs(term))
        total = term if total is None else total + term
        peak = high if peak is None else jnp.maximum(peak, high)
    summed = lax.psum_scatter(
        total.astype(jnp.bfloat16), "dp", scatter_dimension=0, tiled=True, axis_index_groups=lines_of
    )
    grad_peak = lax.pmax(peak, ("dp", "tensor"))
    weight, grad_peak = lax.optimization_barrier((weight, grad_peak))

    grad_input = None
    for step in range(inner):
        folded = jnp.dot(grads[step], weight, preferred_element_type=jnp.float32)
        if moves(step):
            folded = swap(folded.astype(jnp.bfloat16), step).astype(jnp.float32)
        grad_input = folded if grad_input is None else grad_input + folded
    grad_input = grad_input.astype(jnp.bfloat16)

    gradient = summed.astype(jnp.float32)
    squares = lax.psum(jnp.sum(gradient * gradient), ("dp", "tensor"))
    entries = jnp.float32(own * n * cols * lax.axis_size("tensor"))
    clip_factor = jnp.minimum(1.0, jnp.sqrt(entries) / (jnp.sqrt(squares) + 1e-06))
    clipped = clip_factor * gradient
    new_moment = 0.9 * moment + 0.1 * clipped
    new_second = 0.95 * second + 0.05 * clipped * clipped
    new_master = master - 0.01 * (new_moment / (jnp.sqrt(new_second) + 1e-08) + 0.1 * master)
    row_peak = lax.pmax(jnp.max(jnp.abs(new_master), axis=1), "tensor") + 1e-06
    new_codes = (new_master / row_peak[:, None]).astype(jnp.bfloat16)
    new_scales = row_peak.astype(jnp.bfloat16)
    return (grad_input, new_master, new_moment, new_second, new_codes, new_scales, grad_peak)


def solution(mesh):
    n = mesh.shape["dp"]

    def body(*args):
        return on_device(n, *args)

    return jax.shard_map(
        body,
        mesh=mesh,
        in_specs=(
            P("dp", "tensor"),
            P("dp", None),
            P("dp", "tensor"),
            P("dp"),
            P("dp", "tensor"),
            P("dp", "tensor"),
            P("dp", "tensor"),
        ),
        out_specs=(
            P("dp", "tensor"),
            P("dp", "tensor"),
            P("dp", "tensor"),
            P("dp", "tensor"),
            P("dp", "tensor"),
            P("dp"),
            P(),
        ),
        check_vma=False,
    )
```

time: 1900 us -> 756 us (0.40)
  waiting for transfers between devices: 1520 us -> 413 us
  other arithmetic: 112 us -> 55 us
  blocking collectives: 131 us -> 88.2 us
  matrix products: 118 us -> 149 us
    reduce_scatter x1, waiting for transfers between devices: 994 us -> 226 us  [on_device(): lax.psum_scatter(total.astype(jnp.bfloat16), 'dp', scatter_dimension=0, t...]
    all_gather x1, waiting for transfers between devices: 526 us -> 0.01 us  [on_device(): lax.all_gather(weight, 'dp', axis=0, tiled=True, axis_index_groups=lines_of)]
    ppermute x0 -> x9, waiting for transfers between devices: none -> 187 us  [swap(): return lax.ppermute(value, 'dp', pairs)]
    convert_element_type x2 -> x3, other arithmetic: 74.4 us -> 17.8 us  [the longest x1 11.1 us: on_device(): grad_input = grad_input.astype(jnp.bfloat16)]
    all_gather x1 -> x0, blocking collectives: 41.7 us -> none  [on_device(): lax.all_gather(weight_scales, 'dp', axis=0, tiled=True).astype(jnp.float32)]
    dot_general x2 -> x8, matrix products: 118 us -> 149 us  [the longest x4 102 us: on_device(): lax.dot_general(block, act, (((0,), (0,)), ((), ())), preferred_element_t...]
  transfers between devices with their start and end apart: 2 -> 11, of which waited for: 2 -> 2; matrix products, arithmetic and copies ran while one was open for 10% -> 23% of each run, Pallas kernels for 0% -> 0%
where the time goes in v1:
time: 756 us; the launch traced here: 755 us
  waiting for transfers between devices  413 us (55%)
  matrix products  149 us (20%)
  blocking collectives  88.2 us (12%)
  other arithmetic  55 us (7%)
  local copies, waits for them, and re-layouts  18 us (2%)
  between operations  17.4 us (2%)
  starting transfers between devices  14.7 us (2%)
    reduce_scatter x1, waiting for transfers between devices, on_device(): lax.psum_scatter(total.astype(jnp.bfloat16), 'dp', scatter_dimension=0, t...  226 us
    ppermute x9, waiting for transfers between devices, swap(): return lax.ppermute(value, 'dp', pairs)  187 us
    dot_general x4, matrix products, on_device(): lax.dot_general(block, act, (((0,), (0,)), ((), ())), preferred_element_t...  102 us
    dot_general x4, matrix products, on_device(): folded = jnp.dot(grads[step], weight, preferred_element_type=jnp.float32)  46.7 us
    pmax x1, blocking collectives, on_device(): grad_peak = lax.pmax(peak, ('dp', 'tensor'))  44.3 us
    psum x1, blocking collectives, on_device(): squares = lax.psum(jnp.sum(gradient * gradient), ('dp', 'tensor'))  41.4 us
    reduce_max x1, other arithmetic, on_device(): row_peak = lax.pmax(jnp.max(jnp.abs(new_master), axis=1), 'tensor') + 1e-06  24.1 us
  transfers between devices with their start and end apart: 11, of which 2 were waited for; matrix products, arithmetic and copies ran while one was open for 23% of the time, Pallas kernels for 0%

profile of v1, /device:TPU:0, one launch (start us, length us, event | category | flops | bytes accessed | tf_op | source)
XLA Modules:
  0.0 755.2 jit_solution(10425100185984457022)
XLA Ops:
  7.2 0.0 all-gather.2.cloned.1.call-start
  7.2 0.7 convert_element_type.43
  7.9 6.0 multiply_convert_fusion
  13.9 0.0 all-gather.2.cloned.1.call-update
  14.0 0.0 reduce-scatter.2.cloned.1.call-start
  14.0 3.0 collective-permute-start.1
  17.0 1.5 collective-permute-start.3
  18.5 0.0 collective-permute-start.5
  18.6 6.7 copy.14
  25.3 6.2 copy.15
  31.5 4.1 dynamic-slice_bitcast_fusion.1
  35.6 2.0 collective-permute-start
  37.5 1.5 collective-permute-start.2
  39.1 19.2 %fusion.6 = f32[1536,6144]{1,0:T(8,128)} fusion(bf16[384,6144]{1,0:T(8,128)(2,1)} %param.7, bf16[4,384,1536]{1,2,0:T(8,128)(2,1)} %bitcast.30, s32[]{:T(128)S(6)} %select_n.13), kind=kOutput, calls=%fused_computation.22 | convolution fusion | flops 7247757312 | bytes 43646980 | tf_op jit(solution)/shard_map/dot_general | solution.py:51
  58.3 187.2 %collective-permute-done = bf16[384,1536]{0,1:T(8,128)(2,1)S(1)} collective-permute-done((bf16[384,1536]{0,1:T(8,128)(2,1)}, bf16[384,1536]{0,1:T(8,128)(2,1)S(1)}, u32[]{:S(2)}, u32[]{:S(2)}) %collective-permute-start) | collective-permute-done | bytes 1179680 | tf_op jit(solution)/shard_map/ppermute | solution.py:31
  245.5 2.7 collective-permute-start.4
  248.2 0.0 collective-permute-done.1
  248.2 18.1 %fusion.15 = f32[1536,6144]{1,0:T(8,128)} fusion(bf16[384,1536]{0,1:T(8,128)(2,1)S(1)} %collective-permute-done, bf16[384,6144]{1,0:T(8,128)(2,1)} %collective-permute-done.1), kind=kOutput, calls=%fused_computation.33 | convolution fusion | flops 7247757312 | bytes 43646976 | tf_op jit(solution)/shard_map/dot_general | solution.py:51
  266.3 0.0 collective-permute-done.2
  266.3 0.0 collective-permute-done.3
  266.3 18.3 %fusion.16 = f32[1536,6144]{1,0:T(8,128)} fusion(bf16[384,1536]{0,1:T(8,128)(2,1)S(1)} %collective-permute-done.2, bf16[384,6144]{1,0:T(8,128)(2,1)} %collective-permute-done.3), kind=kOutput, calls=%fused_computation.34 | convolution fusion | flops 7247757312 | bytes 43646976 | tf_op jit(solution)/shard_map/dot_general | solution.py:51
  284.5 0.0 collective-permute-done.4
  284.5 0.0 copy-start.1
  284.5 1.0 copy-done.1
  285.6 0.0 collective-permute-done.5
  285.6 46.3 %add_convert_fusion = (bf16[1536,6144]{1,0:T(8,128)(2,1)}, f32[]{:T(128)}, f32[]{:T(128)}, f32[]{:T(128)}, f32[]{:T(128)}) fusion(f32[1536,6144]{1,0:T(8,128)} %fusion.16, f32[1536,6144]{1,0:T(8,128)} %fusion.6, f32[1536,6144]{1,0:T(8,128)} %fusion.15, bf16[384,1536]{0,1:T(8,128)(2,1)} %copy-done.1, bf16[384,6144]{1,0:T(8,128)(2,1)} %collective-permute-done.5), kind=kOutput, calls=%fused_computation | convolution fusion | flops 7361003520 | bytes 138018832 | tf_op jit(solution)/shard_map/dot_general | solution.py:51
  331.8 0.0 reduce-scatter.2.cloned.1.call-update
  334.5 44.3 %pmax.14 = f32[]{:T(128)} all-reduce(f32[]{:T(128)S(6)} %max.15), channel_id=1, replica_groups=mesh['dp'=16,'tensor'=2] {'dp','tensor'}, use_global_device_ids=true, to_apply=%region_4.5 | all-reduce | flops 1 | bytes 8 | tf_op jit(solution)/shard_map/pmax | solution.py:60
  378.8 0.0 all-gather.2.cloned.1.call-done
  378.8 0.0 copy-start
  378.8 16.0 %convolution_convert_fusion.2 = bf16[384,6144]{1,0:T(8,128)(2,1)} fusion(bf16[384,1536]{0,1:T(8,128)(2,1)S(1)} %collective-permute-done, bf16[1536,6144]{1,0:T(8,128)(2,1)} %all-gather.2.cloned.1.call-done), kind=kOutput, calls=%fused_computation.19 | convolution fusion | flops 7250116608 | bytes 24772608 | tf_op jit(solution)/shard_map/dot_general | solution.py:65
  394.8 0.0 copy-start.2
  394.8 2.3 collective-permute-start.6
  397.1 0.0 copy-done
  397.1 9.4 %convolution_convert_fusion.1 = bf16[384,6144]{1,0:T(8,128)(2,1)} fusion(bf16[384,1536]{0,1:T(8,128)(2,1)S(1)} %collective-permute-done.2, bf16[1536,6144]{1,0:T(8,128)(2,1)S(1)} %copy-done), kind=kOutput, calls=%fused_computation.18 | convolution fusion | flops 7250116608 | bytes 24772608 | tf_op jit(solution)/shard_map/dot_general | solution.py:65
  406.5 0.8 collective-permute-start.7
  407.3 0.0 copy-done.2
  407.3 9.4 %convolution_convert_fusion = bf16[384,6144]{1,0:T(8,128)(2,1)} fusion(bf16[384,1536]{0,1:T(8,128)(2,1)S(1)} %copy-done.2, bf16[1536,6144]{1,0:T(8,128)(2,1)S(1)} %copy-done), kind=kOutput, calls=%fused_computation.17 | convolution fusion | flops 7250116608 | bytes 24772608 | tf_op jit(solution)/shard_map/dot_general | solution.py:65
  416.7 0.8 collective-permute-start.8
  417.5 11.9 %fusion.4 = f32[384,6144]{1,0:T(8,128)} fusion(bf16[1536,6144]{1,0:T(8,128)(2,1)S(1)} %copy-done, bf16[4,384,1536]{1,2,0:T(8,128)(2,1)} %bitcast.31, s32[]{:T(128)S(6)} %select_n.13), kind=kOutput, calls=%fused_computation.20 | convolution fusion | flops 7247757312 | bytes 29491204 | tf_op jit(solution)/shard_map/dot_general | solution.py:65
  429.4 226.1 %reduce-scatter.2.cloned.1.call-done = bf16[384,6144]{1,0:T(8,128)(2,1)} async-done(((bf16[1536,6144]{1,0:T(8,128)(2,1)}), bf16[384,6144]{1,0:T(8,128)(2,1)}) %reduce-scatter.2.cloned.1.call-update) | async-done | bytes 4718608 | tf_op jit(solution)/shard_map/reduce_scatter | solution.py:57
  655.4 5.4 fusion.2
  660.8 0.0 collective-permute-done.6
  660.8 0.0 collective-permute-done.7
  660.8 0.0 collective-permute-done.8
  660.8 11.1 %add_convert_fusion.1 = bf16[384,6144]{1,0:T(8,128)(2,1)} fusion(bf16[384,6144]{1,0:T(8,128)(2,1)} %collective-permute-done.8, bf16[384,6144]{1,0:T(8,128)(2,1)} %collective-permute-done.7, f32[384,6144]{1,0:T(8,128)} %fusion.4, bf16[384,6144]{1,0:T(8,128)(2,1)} %collective-permute-done.6), kind=kLoop, calls=%fused_computation.15 | loop fusion | flops 16515072 | bytes 28311552 | tf_op jit(solution)/shard_map/convert_element_type | solution.py:69
  671.9 41.4 %psum.7 = f32[]{:T(128)} all-reduce(f32[]{:T(128)} %fusion.2), channel_id=1, replica_groups=mesh['dp'=16,'tensor'=2] {'dp','tensor'}, use_global_device_ids=true, to_apply=%region_7.8 | all-reduce | flops 1 | bytes 8 | tf_op jit(solution)/shard_map/psum | solution.py:72
  714.1 24.1 %abs_reduce_fusion.4 = (f32[384]{0:T(512)S(1)}, f32[384,6144]{1,0:T(8,128)}, f32[384,6144]{1,0:T(8,128)}, f32[384,6144]{1,0:T(8,128)}) fusion(f32[384,6144]{1,0:T(8,128)} %param.11, bf16[384,6144]{1,0:T(8,128)(2,1)} %reduce-scatter.2.cloned.1.call-done, f32[]{:T(128)S(6)} %min_shard_map.3, f32[384,6144]{1,0:T(8,128)} %param.13, f32[384,6144]{1,0:T(8,128)} %param.12), kind=kLoop, calls=%fused_computation.13 | loop fusion | flops 40107648 | bytes 61343236 | tf_op jit(solution)/shard_map/reduce_max | solution.py:79
  738.1 2.4 pmax.15
  740.6 0.6 fusion.12
  741.1 7.2 divide_convert_fusion
Async XLA Ops:
  7.2 371.6 %all-gather.2.cloned.1.call-start = ((), (), s32[]{:S(2)}) async-start(), calls=%async_computation.1 | async-start | bytes 23592960 | tf_op jit(solution)/shard_map/all_gather | solution.py:37
  14.0 641.5 %reduce-scatter.2.cloned.1.call-start = ((), (), s32[]{:S(2)}) async-start(), calls=%async_computation.2 | async-start | bytes 23592960 | tf_op jit(solution)/shard_map/reduce_scatter | solution.py:57
  14.0 234.2 %collective-permute-start.1 = (bf16[384,6144]{1,0:T(8,128)(2,1)}, bf16[384,6144]{1,0:T(8,128)(2,1)}, u32[]{:S(2)}, u32[]{:S(2)}) collective-permute-start(bf16[384,6144]{1,0:T(8,128)(2,1)} %param.7), channel_id=1, source_target_pairs={{0,2},{2,0},{4,6},{6,4},{8,10},{10,8},{12,14},{14,12},{16,18},{18,... | collective-permute-start | bytes 14155784 | tf_op jit(solution)/shard_map/ppermute | solution.py:31
  17.0 249.3 %collective-permute-start.3 = (bf16[384,6144]{1,0:T(8,128)(2,1)}, bf16[384,6144]{1,0:T(8,128)(2,1)}, u32[]{:S(2)}, u32[]{:S(2)}) collective-permute-start(bf16[384,6144]{1,0:T(8,128)(2,1)} %param.7), channel_id=1, source_target_pairs={{0,4},{2,6},{4,0},{6,2},{8,12},{10,14},{12,8},{14,10},{16,20},{18,... | collective-permute-start | bytes 14155784 | tf_op jit(solution)/shard_map/ppermute | solution.py:31
  18.5 267.0 %collective-permute-start.5 = (bf16[384,6144]{1,0:T(8,128)(2,1)}, bf16[384,6144]{1,0:T(8,128)(2,1)}, u32[]{:S(2)}, u32[]{:S(2)}) collective-permute-start(bf16[384,6144]{1,0:T(8,128)(2,1)} %param.7), channel_id=1, source_target_pairs={{0,6},{2,4},{4,2},{6,0},{8,14},{10,12},{12,10},{14,8},{16,22},{18,... | collective-permute-start | bytes 14155784 | tf_op jit(solution)/shard_map/ppermute | solution.py:31
  35.6 209.9 %collective-permute-start = (bf16[384,1536]{0,1:T(8,128)(2,1)}, bf16[384,1536]{0,1:T(8,128)(2,1)S(1)}, u32[]{:S(2)}, u32[]{:S(2)}) collective-permute-start(bf16[384,1536]{0,1:T(8,128)(2,1)} %get-tuple-element.22), channel_id=1, source_target_pairs={{0,2},{2,0},{4,6},{6,4},{8,10},{10,8},{12,14},{14,12},{16,18},{18,... | collective-permute-start | bytes 3538952 | tf_op jit(solution)/shard_map/ppermute | solution.py:31
  37.5 228.7 %collective-permute-start.2 = (bf16[384,1536]{0,1:T(8,128)(2,1)}, bf16[384,1536]{0,1:T(8,128)(2,1)S(1)}, u32[]{:S(2)}, u32[]{:S(2)}) collective-permute-start(bf16[384,1536]{0,1:T(8,128)(2,1)} %get-tuple-element.20), channel_id=1, source_target_pairs={{0,4},{2,6},{4,0},{6,2},{8,12},{10,14},{12,8},{14,10},{16,20},{18,... | collective-permute-start | bytes 3538952 | tf_op jit(solution)/shard_map/ppermute | solution.py:31
  245.5 39.1 %collective-permute-start.4 = (bf16[384,1536]{0,1:T(8,128)(2,1)S(1)}, bf16[384,1536]{0,1:T(8,128)(2,1)S(1)}, u32[]{:S(2)}, u32[]{:S(2)}) collective-permute-start(bf16[384,1536]{0,1:T(8,128)(2,1)S(1)} %get-tuple-element.21), channel_id=1, source_target_pairs={{0,6},{2,4},{4,2},{6,0},{8,14},{10,12},{12,10},{14,8},{16,22},{18,... | collective-permute-start | bytes 3538952 | tf_op jit(solution)/shard_map/ppermute | solution.py:31
  284.5 1.0 copy-start.1
  378.8 18.3 %copy-start = (bf16[1536,6144]{1,0:T(8,128)(2,1)S(1)}, bf16[1536,6144]{1,0:T(8,128)(2,1)}, u32[]{:S(2)}) copy-start(bf16[1536,6144]{1,0:T(8,128)(2,1)} %all-gather.2.cloned.1.call-done) | copy-start | bytes 56623108
  394.8 12.5 %copy-start.2 = (bf16[384,1536]{0,1:T(8,128)(2,1)S(1)}, bf16[384,1536]{0,1:T(8,128)(2,1)}, u32[]{:S(2)}) copy-start(bf16[384,1536]{0,1:T(8,128)(2,1)} %copy-done.1) | copy-start | bytes 3538948
  394.8 266.0 %collective-permute-start.6 = (bf16[384,6144]{1,0:T(8,128)(2,1)}, bf16[384,6144]{1,0:T(8,128)(2,1)}, u32[]{:S(2)}, u32[]{:S(2)}) collective-permute-start(bf16[384,6144]{1,0:T(8,128)(2,1)} %convolution_convert_fusion.2), channel_id=1, source_target_pairs={{0,2},{2,0},{4,6},{6,4},{8,10},{10,8},{12,14},{14,12},{16,18},{18,... | collective-permute-start | bytes 14155784 | tf_op jit(solution)/shard_map/ppermute | solution.py:31
  406.5 254.3 %collective-permute-start.7 = (bf16[384,6144]{1,0:T(8,128)(2,1)}, bf16[384,6144]{1,0:T(8,128)(2,1)}, u32[]{:S(2)}, u32[]{:S(2)}) collective-permute-start(bf16[384,6144]{1,0:T(8,128)(2,1)} %convolution_convert_fusion.1), channel_id=1, source_target_pairs={{0,4},{2,6},{4,0},{6,2},{8,12},{10,14},{12,8},{14,10},{16,20},{18,... | collective-permute-start | bytes 14155784 | tf_op jit(solution)/shard_map/ppermute | solution.py:31
  416.7 244.1 %collective-permute-start.8 = (bf16[384,6144]{1,0:T(8,128)(2,1)}, bf16[384,6144]{1,0:T(8,128)(2,1)}, u32[]{:S(2)}, u32[]{:S(2)}) collective-permute-start(bf16[384,6144]{1,0:T(8,128)(2,1)} %convolution_convert_fusion), channel_id=1, source_target_pairs={{0,6},{2,4},{4,2},{6,0},{8,14},{10,12},{12,10},{14,8},{16,22},{18,... | collective-permute-start | bytes 14155784 | tf_op jit(solution)/shard_map/ppermute | solution.py:31
Sparse Core Ops, SparseCore 0:
  14.1 325.2 all-gather.1
  341.8 313.6 reduce-scatter.1

commit v2 on v1

--- a/solution.py
+++ b/solution.py
@@ -69,7 +69,12 @@
     grad_input = grad_input.astype(jnp.bfloat16)
 
     gradient = summed.astype(jnp.float32)
-    squares = lax.psum(jnp.sum(gradient * gradient), ("dp", "tensor"))
+    squares = lax.psum(jnp.sum(gradient * gradient), "tensor")
+    if n & (n - 1) == 0:
+        for bit in range(n.bit_length() - 1):
+            squares += lax.ppermute(squares, "dp", [(i, i ^ (1 << bit)) for i in range(n)])
+    else:
+        squares = lax.psum(squares, "dp")
     entries = jnp.float32(own * n * cols * lax.axis_size("tensor"))
     clip_factor = jnp.minimum(1.0, jnp.sqrt(entries) / (jnp.sqrt(squares) + 1e-06))
     clipped = clip_factor * gradient

time: 756 us -> 736 us (0.974)
  blocking collectives: 88.2 us -> 49.8 us
  starting transfers between devices: 14.7 us -> 25.7 us
    psum x1, blocking collectives: 41.4 us -> 3.08 us  [on_device(): squares = lax.psum(jnp.sum(gradient * gradient), 'tensor')]
    ppermute x0 -> x4, starting transfers between devices: none -> 11 us  [on_device(): lax.ppermute(squares, 'dp', [(i, i ^ 1 << bit) for i in range(n)])]
  transfers between devices with their start and end apart: 11 -> 15, of which waited for: 2 -> 6; matrix products, arithmetic and copies ran while one was open for 23% -> 23% of each run, Pallas kernels for 0% -> 0%
where the time goes in v2:
time: 736 us; the launch traced here: 735 us
  waiting for transfers between devices  419 us (57%)
  matrix products  149 us (20%)
  other arithmetic  55 us (7%)
  blocking collectives  49.8 us (7%)
  starting transfers between devices  25.7 us (3%)
  between operations  19.6 us (3%)
  local copies, waits for them, and re-layouts  18 us (2%)
    reduce_scatter x1, waiting for transfers between devices, on_device(): lax.psum_scatter(total.astype(jnp.bfloat16), 'dp', scatter_dimension=0, t...  226 us
    ppermute x9, waiting for transfers between devices, swap(): return lax.ppermute(value, 'dp', pairs)  187 us
    dot_general x4, matrix products, on_device(): lax.dot_general(block, act, (((0,), (0,)), ((), ())), preferred_element_t...  102 us
    dot_general x4, matrix products, on_device(): folded = jnp.dot(grads[step], weight, preferred_element_type=jnp.float32)  46.7 us
    pmax x1, blocking collectives, on_device(): grad_peak = lax.pmax(peak, ('dp', 'tensor'))  44.3 us
    reduce_max x1, other arithmetic, on_device(): row_peak = lax.pmax(jnp.max(jnp.abs(new_master), axis=1), 'tensor') + 1e-06  24.1 us
  transfers between devices with their start and end apart: 15, of which 6 were waited for; matrix products, arithmetic and copies ran while one was open for 23% of the time, Pallas kernels for 0%

profile of v2, /device:TPU:0, one launch (start us, length us, event | category | flops | bytes accessed | tf_op | source)
XLA Modules:
  0.0 735.4 jit_solution(13760779817993110295)
XLA Ops:
  7.2 0.0 all-gather.2.cloned.1.call-start
  7.2 0.7 convert_element_type.43
  7.9 6.0 multiply_convert_fusion
  13.9 0.0 all-gather.2.cloned.1.call-update
  14.0 0.0 reduce-scatter.2.cloned.1.call-start
  14.0 3.0 collective-permute-start.1
  17.0 1.5 collective-permute-start.3
  18.5 0.0 collective-permute-start.5
  18.6 6.7 copy.14
  25.3 6.2 copy.15
  31.5 4.1 dynamic-slice_bitcast_fusion.1
  35.6 2.0 collective-permute-start
  37.5 1.5 collective-permute-start.2
  39.1 19.2 %fusion.6 = f32[1536,6144]{1,0:T(8,128)} fusion(bf16[384,6144]{1,0:T(8,128)(2,1)} %param.7, bf16[4,384,1536]{1,2,0:T(8,128)(2,1)} %bitcast.30, s32[]{:T(128)S(6)} %select_n.13), kind=kOutput, calls=%fused_computation.22 | convolution fusion | flops 7247757312 | bytes 43646980 | tf_op jit(solution)/shard_map/dot_general | solution.py:51
  58.3 187.2 %collective-permute-done = bf16[384,1536]{0,1:T(8,128)(2,1)S(1)} collective-permute-done((bf16[384,1536]{0,1:T(8,128)(2,1)}, bf16[384,1536]{0,1:T(8,128)(2,1)S(1)}, u32[]{:S(2)}, u32[]{:S(2)}) %collective-permute-start) | collective-permute-done | bytes 1179680 | tf_op jit(solution)/shard_map/ppermute | solution.py:31
  245.5 2.7 collective-permute-start.4
  248.2 0.0 collective-permute-done.1
  248.2 18.1 %fusion.15 = f32[1536,6144]{1,0:T(8,128)} fusion(bf16[384,1536]{0,1:T(8,128)(2,1)S(1)} %collective-permute-done, bf16[384,6144]{1,0:T(8,128)(2,1)} %collective-permute-done.1), kind=kOutput, calls=%fused_computation.33 | convolution fusion | flops 7247757312 | bytes 43646976 | tf_op jit(solution)/shard_map/dot_general | solution.py:51
  266.3 0.0 collective-permute-done.2
  266.3 0.0 collective-permute-done.3
  266.3 18.3 %fusion.16 = f32[1536,6144]{1,0:T(8,128)} fusion(bf16[384,1536]{0,1:T(8,128)(2,1)S(1)} %collective-permute-done.2, bf16[384,6144]{1,0:T(8,128)(2,1)} %collective-permute-done.3), kind=kOutput, calls=%fused_computation.34 | convolution fusion | flops 7247757312 | bytes 43646976 | tf_op jit(solution)/shard_map/dot_general | solution.py:51
  284.5 0.0 collective-permute-done.4
  284.5 0.0 copy-start.1
  284.5 1.0 copy-done.1
  285.6 0.0 collective-permute-done.5
  285.6 46.3 %add_convert_fusion = (bf16[1536,6144]{1,0:T(8,128)(2,1)}, f32[]{:T(128)}, f32[]{:T(128)}, f32[]{:T(128)}, f32[]{:T(128)}) fusion(f32[1536,6144]{1,0:T(8,128)} %fusion.16, f32[1536,6144]{1,0:T(8,128)} %fusion.6, f32[1536,6144]{1,0:T(8,128)} %fusion.15, bf16[384,1536]{0,1:T(8,128)(2,1)} %copy-done.1, bf16[384,6144]{1,0:T(8,128)(2,1)} %collective-permute-done.5), kind=kOutput, calls=%fused_computation | convolution fusion | flops 7361003520 | bytes 138018832 | tf_op jit(solution)/shard_map/dot_general | solution.py:51
  331.8 0.0 reduce-scatter.2.cloned.1.call-update
  334.5 44.3 %pmax.14 = f32[]{:T(128)} all-reduce(f32[]{:T(128)S(6)} %max.15), channel_id=1, replica_groups=mesh['dp'=16,'tensor'=2] {'dp','tensor'}, use_global_device_ids=true, to_apply=%region_4.5 | all-reduce | flops 1 | bytes 8 | tf_op jit(solution)/shard_map/pmax | solution.py:60
  378.8 0.0 all-gather.2.cloned.1.call-done
  378.8 0.0 copy-start
  378.8 16.0 %convolution_convert_fusion.2 = bf16[384,6144]{1,0:T(8,128)(2,1)} fusion(bf16[384,1536]{0,1:T(8,128)(2,1)S(1)} %collective-permute-done, bf16[1536,6144]{1,0:T(8,128)(2,1)} %all-gather.2.cloned.1.call-done), kind=kOutput, calls=%fused_computation.19 | convolution fusion | flops 7250116608 | bytes 24772608 | tf_op jit(solution)/shard_map/dot_general | solution.py:65
  394.8 0.0 copy-start.2
  394.8 2.3 collective-permute-start.6
  397.1 0.0 copy-done
  397.1 9.4 %convolution_convert_fusion.1 = bf16[384,6144]{1,0:T(8,128)(2,1)} fusion(bf16[384,1536]{0,1:T(8,128)(2,1)S(1)} %collective-permute-done.2, bf16[1536,6144]{1,0:T(8,128)(2,1)S(1)} %copy-done), kind=kOutput, calls=%fused_computation.18 | convolution fusion | flops 7250116608 | bytes 24772608 | tf_op jit(solution)/shard_map/dot_general | solution.py:65
  406.5 0.8 collective-permute-start.7
  407.3 0.0 copy-done.2
  407.3 9.4 %convolution_convert_fusion = bf16[384,6144]{1,0:T(8,128)(2,1)} fusion(bf16[384,1536]{0,1:T(8,128)(2,1)S(1)} %copy-done.2, bf16[1536,6144]{1,0:T(8,128)(2,1)S(1)} %copy-done), kind=kOutput, calls=%fused_computation.17 | convolution fusion | flops 7250116608 | bytes 24772608 | tf_op jit(solution)/shard_map/dot_general | solution.py:65
  416.7 0.8 collective-permute-start.8
  417.5 11.9 %fusion.4 = f32[384,6144]{1,0:T(8,128)} fusion(bf16[1536,6144]{1,0:T(8,128)(2,1)S(1)} %copy-done, bf16[4,384,1536]{1,2,0:T(8,128)(2,1)} %bitcast.31, s32[]{:T(128)S(6)} %select_n.13), kind=kOutput, calls=%fused_computation.20 | convolution fusion | flops 7247757312 | bytes 29491204 | tf_op jit(solution)/shard_map/dot_general | solution.py:65
  429.4 226.1 %reduce-scatter.2.cloned.1.call-done = bf16[384,6144]{1,0:T(8,128)(2,1)} async-done(((bf16[1536,6144]{1,0:T(8,128)(2,1)}), bf16[384,6144]{1,0:T(8,128)(2,1)}) %reduce-scatter.2.cloned.1.call-update) | async-done | bytes 4718608 | tf_op jit(solution)/shard_map/reduce_scatter | solution.py:57
  655.4 5.4 fusion.2
  660.8 0.0 collective-permute-done.6
  660.8 0.0 collective-permute-done.7
  660.8 0.0 collective-permute-done.8
  660.8 11.1 %add_convert_fusion.1 = bf16[384,6144]{1,0:T(8,128)(2,1)} fusion(bf16[384,6144]{1,0:T(8,128)(2,1)} %collective-permute-done.8, bf16[384,6144]{1,0:T(8,128)(2,1)} %collective-permute-done.7, f32[384,6144]{1,0:T(8,128)} %fusion.4, bf16[384,6144]{1,0:T(8,128)(2,1)} %collective-permute-done.6), kind=kLoop, calls=%fused_computation.15 | loop fusion | flops 16515072 | bytes 28311552 | tf_op jit(solution)/shard_map/convert_element_type | solution.py:69
  671.9 3.1 psum.7
  675.0 1.5 collective-permute-start.9
  676.5 2.3 collective-permute-done.9
  680.0 2.8 collective-permute-start.10
  682.8 0.9 collective-permute-done.10
  684.2 1.8 collective-permute-start.11
  686.1 1.9 collective-permute-done.11
  688.5 4.9 collective-permute-start.12
  693.4 0.3 collective-permute-done.12
  694.3 24.1 %abs_reduce_fusion.4 = (f32[384]{0:T(512)S(1)}, f32[384,6144]{1,0:T(8,128)}, f32[384,6144]{1,0:T(8,128)}, f32[384,6144]{1,0:T(8,128)}) fusion(f32[384,6144]{1,0:T(8,128)} %param.11, bf16[384,6144]{1,0:T(8,128)(2,1)} %reduce-scatter.2.cloned.1.call-done, f32[]{:T(128)S(6)} %min_shard_map.3, f32[384,6144]{1,0:T(8,128)} %param.13, f32[384,6144]{1,0:T(8,128)} %param.12), kind=kLoop, calls=%fused_computation.13 | loop fusion | flops 40107648 | bytes 61343236 | tf_op jit(solution)/shard_map/reduce_max | solution.py:84
  718.4 2.4 pmax.15
  720.8 0.6 fusion.12
  721.4 7.2 divide_convert_fusion
Async XLA Ops:
  7.2 371.6 %all-gather.2.cloned.1.call-start = ((), (), s32[]{:S(2)}) async-start(), calls=%async_computation.1 | async-start | bytes 23592960 | tf_op jit(solution)/shard_map/all_gather | solution.py:37
  14.0 641.5 %reduce-scatter.2.cloned.1.call-start = ((), (), s32[]{:S(2)}) async-start(), calls=%async_computation.2 | async-start | bytes 23592960 | tf_op jit(solution)/shard_map/reduce_scatter | solution.py:57
  14.0 234.2 %collective-permute-start.1 = (bf16[384,6144]{1,0:T(8,128)(2,1)}, bf16[384,6144]{1,0:T(8,128)(2,1)}, u32[]{:S(2)}, u32[]{:S(2)}) collective-permute-start(bf16[384,6144]{1,0:T(8,128)(2,1)} %param.7), channel_id=1, source_target_pairs={{0,2},{2,0},{4,6},{6,4},{8,10},{10,8},{12,14},{14,12},{16,18},{18,... | collective-permute-start | bytes 14155784 | tf_op jit(solution)/shard_map/ppermute | solution.py:31
  17.0 249.3 %collective-permute-start.3 = (bf16[384,6144]{1,0:T(8,128)(2,1)}, bf16[384,6144]{1,0:T(8,128)(2,1)}, u32[]{:S(2)}, u32[]{:S(2)}) collective-permute-start(bf16[384,6144]{1,0:T(8,128)(2,1)} %param.7), channel_id=1, source_target_pairs={{0,4},{2,6},{4,0},{6,2},{8,12},{10,14},{12,8},{14,10},{16,20},{18,... | collective-permute-start | bytes 14155784 | tf_op jit(solution)/shard_map/ppermute | solution.py:31
  18.5 267.0 %collective-permute-start.5 = (bf16[384,6144]{1,0:T(8,128)(2,1)}, bf16[384,6144]{1,0:T(8,128)(2,1)}, u32[]{:S(2)}, u32[]{:S(2)}) collective-permute-start(bf16[384,6144]{1,0:T(8,128)(2,1)} %param.7), channel_id=1, source_target_pairs={{0,6},{2,4},{4,2},{6,0},{8,14},{10,12},{12,10},{14,8},{16,22},{18,... | collective-permute-start | bytes 14155784 | tf_op jit(solution)/shard_map/ppermute | solution.py:31
  35.6 209.9 %collective-permute-start = (bf16[384,1536]{0,1:T(8,128)(2,1)}, bf16[384,1536]{0,1:T(8,128)(2,1)S(1)}, u32[]{:S(2)}, u32[]{:S(2)}) collective-permute-start(bf16[384,1536]{0,1:T(8,128)(2,1)} %get-tuple-element.22), channel_id=1, source_target_pairs={{0,2},{2,0},{4,6},{6,4},{8,10},{10,8},{12,14},{14,12},{16,18},{18,... | collective-permute-start | bytes 3538952 | tf_op jit(solution)/shard_map/ppermute | solution.py:31
  37.5 228.7 %collective-permute-start.2 = (bf16[384,1536]{0,1:T(8,128)(2,1)}, bf16[384,1536]{0,1:T(8,128)(2,1)S(1)}, u32[]{:S(2)}, u32[]{:S(2)}) collective-permute-start(bf16[384,1536]{0,1:T(8,128)(2,1)} %get-tuple-element.20), channel_id=1, source_target_pairs={{0,4},{2,6},{4,0},{6,2},{8,12},{10,14},{12,8},{14,10},{16,20},{18,... | collective-permute-start | bytes 3538952 | tf_op jit(solution)/shard_map/ppermute | solution.py:31
  245.5 39.1 %collective-permute-start.4 = (bf16[384,1536]{0,1:T(8,128)(2,1)S(1)}, bf16[384,1536]{0,1:T(8,128)(2,1)S(1)}, u32[]{:S(2)}, u32[]{:S(2)}) collective-permute-start(bf16[384,1536]{0,1:T(8,128)(2,1)S(1)} %get-tuple-element.21), channel_id=1, source_target_pairs={{0,6},{2,4},{4,2},{6,0},{8,14},{10,12},{12,10},{14,8},{16,22},{18,... | collective-permute-start | bytes 3538952 | tf_op jit(solution)/shard_map/ppermute | solution.py:31
  284.5 1.0 copy-start.1
  378.8 18.3 %copy-start = (bf16[1536,6144]{1,0:T(8,128)(2,1)S(1)}, bf16[1536,6144]{1,0:T(8,128)(2,1)}, u32[]{:S(2)}) copy-start(bf16[1536,6144]{1,0:T(8,128)(2,1)} %all-gather.2.cloned.1.call-done) | copy-start | bytes 56623108
  394.8 12.5 %copy-start.2 = (bf16[384,1536]{0,1:T(8,128)(2,1)S(1)}, bf16[384,1536]{0,1:T(8,128)(2,1)}, u32[]{:S(2)}) copy-start(bf16[384,1536]{0,1:T(8,128)(2,1)} %copy-done.1) | copy-start | bytes 3538948
  394.8 266.0 %collective-permute-start.6 = (bf16[384,6144]{1,0:T(8,128)(2,1)}, bf16[384,6144]{1,0:T(8,128)(2,1)}, u32[]{:S(2)}, u32[]{:S(2)}) collective-permute-start(bf16[384,6144]{1,0:T(8,128)(2,1)} %convolution_convert_fusion.2), channel_id=1, source_target_pairs={{0,2},{2,0},{4,6},{6,4},{8,10},{10,8},{12,14},{14,12},{16,18},{18,... | collective-permute-start | bytes 14155784 | tf_op jit(solution)/shard_map/ppermute | solution.py:31
  406.5 254.3 %collective-permute-start.7 = (bf16[384,6144]{1,0:T(8,128)(2,1)}, bf16[384,6144]{1,0:T(8,128)(2,1)}, u32[]{:S(2)}, u32[]{:S(2)}) collective-permute-start(bf16[384,6144]{1,0:T(8,128)(2,1)} %convolution_convert_fusion.1), channel_id=1, source_target_pairs={{0,4},{2,6},{4,0},{6,2},{8,12},{10,14},{12,8},{14,10},{16,20},{18,... | collective-permute-start | bytes 14155784 | tf_op jit(solution)/shard_map/ppermute | solution.py:31
  416.7 244.1 %collective-permute-start.8 = (bf16[384,6144]{1,0:T(8,128)(2,1)}, bf16[384,6144]{1,0:T(8,128)(2,1)}, u32[]{:S(2)}, u32[]{:S(2)}) collective-permute-start(bf16[384,6144]{1,0:T(8,128)(2,1)} %convolution_convert_fusion), channel_id=1, source_target_pairs={{0,6},{2,4},{4,2},{6,0},{8,14},{10,12},{12,10},{14,8},{16,22},{18,... | collective-permute-start | bytes 14155784 | tf_op jit(solution)/shard_map/ppermute | solution.py:31
  675.0 3.8 collective-permute-start.9
  680.0 3.7 collective-permute-start.10
  684.2 3.7 collective-permute-start.11
  688.5 5.2 collective-permute-start.12
Sparse Core Ops, SparseCore 0:
  14.1 325.2 all-gather.1
  341.8 313.6 reduce-scatter.1
